TPU v7x, 512 devices: a whole 4x8x8 slice. The times are simulated.
512 devices in a mesh: cls: 16 (over z, core), dir: 32 (over y, x).
Axes of the slice: x: 4, y: 8, z: 8, core: 2. Of those that a mesh axis runs over, the one named last changes fastest.
Arguments:
- particles: bfloat16 [256, 4224], P('cls', 'dir')
- assignments: int32 [256, 1], P('cls'), may hold values from 0 to 15; in each aligned block of 16 rows (0 to 15, 16 to 31, ...) at most 3 rows name the same one
- defocus_bins: int32 [256], P('cls'), may hold values from 0 to 63
- ctf_table: float32 [64, 33], replicated, may hold values from -1 to 1
- references: bfloat16 [16, 4608, 4224], P('cls', 'dir'), may hold values from -6 to 6
Outputs:
- best_score: float32 [256], P('cls')
- normalized: float32 [256], P('cls')
Inputs may be any that keep to these rules, and one draw needn't show every extreme that they name: `assignments`: among the 16 particles of one index of cls no class is named more than 3 times; one class is named exactly 3 times in some of them.
All inputs are finite; a program needn't handle non-finite values.
Results may differ from a plain program's by a relative error of at most 0.0017.
Values may be sent and summed in bfloat16 or wider, within the bound.
A program may use at most 64 MiB of HBM per device.

v0:
```python
import math

import jax
import jax.numpy as jnp
from jax import lax
from jax.sharding import PartitionSpec as P

CYCLES = 33
ANGLES = 64
ROTS = 16


def on_device(particles, assignments, defocus_bins, ctf_table, references):
    classes = lax.axis_size("cls")
    row_count = particles.shape[0]
    capacity = 3 * row_count // classes
    slot_count = classes * capacity
    templates = references[0]
    dir_count, features = templates.shape
    bin_count = ctf_table.shape[0]
    assign = assignments[:, 0]
    onehot = (assign[:, None] == jnp.arange(classes, dtype=jnp.int32)[None, :]).astype(jnp.int32)
    placing = jnp.sum((jnp.cumsum(onehot, axis=0) - onehot) * onehot, axis=1)
    slot_index = assign * capacity + placing
    dispatch = (slot_index[None, :] == jnp.arange(slot_count, dtype=jnp.int32)[:, None]).astype(
        jnp.float32
    )
    dispatch_half = dispatch.astype(jnp.bfloat16)
    bins_sent = jnp.dot(dispatch, defocus_bins.astype(jnp.float32), precision=lax.Precision.HIGHEST)
    bins_sent = bins_sent.astype(jnp.bfloat16).reshape(classes, capacity)
    packed = jnp.dot(dispatch_half, particles, preferred_element_type=jnp.float32).astype(
        jnp.bfloat16
    )
    packed = packed.reshape(classes, capacity, particles.shape[1])
    arrived, bins_got = (
        lax.all_to_all(packed, "cls", split_axis=0, concat_axis=0, tiled=True),
        lax.all_to_all(bins_sent, "cls", split_axis=0, concat_axis=0, tiled=True),
    )
    panels = lax.all_gather(arrived, "dir", axis=2, tiled=True)
    panels = panels.reshape(slot_count, CYCLES, 2 * ANGLES)
    bins_got = bins_got.reshape(slot_count).astype(jnp.float32)
    bin_onehot = (bins_got[:, None] == jnp.arange(bin_count, dtype=jnp.float32)[None, :]).astype(
        jnp.float32
    )
    ctf_rows = jnp.dot(bin_onehot, ctf_table, precision=lax.Precision.HIGHEST)
    shaped_templates = templates.reshape(dir_count, CYCLES, 2 * ANGLES)
    energy = jnp.einsum(
        "dra,dra->dr", shaped_templates, shaped_templates, preferred_element_type=jnp.float32
    )
    penalty = 0.5 * jnp.dot(ctf_rows * ctf_rows, energy.T, precision=lax.Precision.HIGHEST)
    weighted = (panels * ctf_rows[:, :, None]).astype(jnp.bfloat16)
    block_rows = 48
    block_count = slot_count // block_rows
    weighted = weighted.reshape(block_count, block_rows, CYCLES, 2 * ANGLES)
    penalty = penalty.reshape(block_count, block_rows, dir_count)
    scale = 1.0 / math.sqrt(features / 3.0)
    stride = 2 * (ANGLES // ROTS)

    def block_best(inputs):
        block_weighted, block_penalty = inputs
        turned = jnp.stack(
            [jnp.roll(block_weighted, rotation * stride, axis=2) for rotation in range(ROTS)],
            axis=1,
        )
        turned = turned.reshape(block_rows * ROTS, features)
        cross = lax.dot_general(
            templates, turned, (((1,), (1,)), ((), ())), preferred_element_type=jnp.float32
        )
        cross = cross.reshape(dir_count, block_rows, ROTS)
        score = (cross - block_penalty.T[:, :, None]) * scale
        return jnp.max(score, axis=(0, 2))

    local_best = lax.map(block_best, (weighted, penalty)).reshape(slot_count)
    group_best = lax.pmax(local_best, "dir")
    returned = lax.all_to_all(
        group_best.reshape(classes, capacity), "cls", split_axis=0, concat_axis=0, tiled=True
    )
    own_best = jnp.dot(dispatch.T, returned.reshape(slot_count), precision=lax.Precision.HIGHEST)
    spread = lax.psum(jnp.sum(own_best * own_best), "cls")
    normalized = own_best / jnp.sqrt(spread / (row_count * classes) + 1e-05)
    return (own_best, normalized)


def solution(mesh):
    placed = (P("cls", "dir"), P("cls", None), P("cls"), P(), P("cls", "dir", None))
    return jax.shard_map(
        on_device, mesh=mesh, in_specs=placed, out_specs=(P("cls"), P("cls")), check_vma=False
    )
```

profile of v0, /device:TPU:1, one launch (start us, length us, event | category | flops | bytes accessed | tf_op | source)
XLA Modules:
  0.0 236.1 jit_solution(4397606471527722931)
XLA Ops:
  0.6 0.7 fusion.47
  1.4 0.8 select_reduce_fusion
  2.3 0.7 multiply_add_fusion
  2.9 0.8 fusion.25
  3.7 0.7 all_to_all.20
  4.4 11.8 %all-to-all-start.1 = ((bf16[16,1,3]{2,1,0:T(2,128)(2,1)}), bf16[16,1,3]{2,1,0:T(2,128)(2,1)S(1)}, u32[]{:S(2)}, u32[]{:S(2)}) async-start(bf16[16,1,3]{2,1,0:T(2,128)(2,1)} %all_to_all.20), calls=%async_computation.1 | async-start | bytes 16384 | tf_op jit(solution)/shard_map/all_to_all | solution.py:37
  16.2 0.8 convolution_convert_fusion
  17.1 2.3 reshape_squeeze.3
  19.4 0.8 fusion.3
  20.2 0.7 reshape.103
  20.9 2.3 all-to-all-done.1
  23.3 4.9 %all-to-all-start = ((bf16[16,2,198]{2,1,0:T(2,128)(2,1)}), bf16[16,2,198]{2,1,0:T(2,128)(2,1)S(1)}, u32[]{:S(2)}, u32[]{:S(2)}) async-start(bf16[16,2,198]{2,1,0:T(2,128)(2,1)} %reshape.103), calls=%async_computation | async-start | bytes 32768 | tf_op jit(solution)/shard_map/all_to_all | solution.py:36
  29.2 6.3 %all-to-all-done = bf16[16,2,198]{2,1,0:T(2,128)(2,1)S(1)} async-done(((bf16[16,2,198]{2,1,0:T(2,128)(2,1)}), bf16[16,2,198]{2,1,0:T(2,128)(2,1)S(1)}, u32[]{:S(2)}, u32[]{:S(2)}) %all-to-all-start) | async-done | bytes 12704 | tf_op jit(solution)/shard_map/all_to_all | solution.py:36
  35.8 51.0 %all_gather.3 = bf16[16,3,4224]{0,1,2:T(4,128)(2,1)} all-gather(bf16[16,3,132]{0,1,2:T(4,128)(2,1)S(1)} %copy.23), channel_id=1, replica_groups=mesh['cls'=16,'dir'=32] {'dir'}, dimensions={2}, use_global_device_ids=true | all-gather | bytes 418176 | tf_op jit(solution)/shard_map/all_gather | solution.py:39
  86.8 5.6 %copy.24 = bf16[16,3,4224]{2,0,1:T(8,128)(2,1)S(1)} copy(bf16[16,3,4224]{0,1,2:T(4,128)(2,1)} %all_gather.3) | data formatting | bytes 811008 | tf_op jit(solution)/shard_map/all_gather | solution.py:39
  92.6 0.4 reshape.81
  93.3 0.9 fusion.49
  94.3 1.1 fusion.50
  95.4 0.4 reshape.79
  99.0 0.4 fusion.27
  99.3 0.4 fusion.28
  100.1 0.4 fusion.30
  100.9 0.4 fusion.32
  104.7 5.3 %copy.30 = bf16[48,16,33,128]{3,2,1,0:T(8,128)(2,1)} copy(bf16[48,16,33,128]{3,2,0,1:T(8,128)(2,1)S(1)} %fusion.41) | data formatting | bytes 12976128 | tf_op jit(solution)/shard_map/while/body/eval_jaxpr/stack | solution.py:61
  110.0 5.2 %fusion.20 = f32[768]{0:T(1024)S(1)} fusion(f32[144,768]{1,0:T(8,128)S(1)} %copy.31, bf16[1,144,4224]{2,1,0:T(8,128)(2,1)S(1)} %copy-done.4, bf16[96,8,33,128]{3,2,1,0:T(8,128)(2,1)} %bitcast.109), kind=kOutput, calls=%fused_computation.9 | convolution fusion | flops 934612224 | bytes 8150016 | tf_op jit(solution)/shard_map/while/body/eval_jaxpr/dot_general | solution.py:66
  115.5 59.0 %pmax.7 = f32[16,1,3]{2,0,1:T(8,128)S(1)} all-reduce(f32[16,1,3]{2,0,1:T(8,128)S(1)} %all_to_all.18), channel_id=1, replica_groups=mesh['cls'=16,'dir'=32] {'dir'}, use_global_device_ids=true, to_apply=%region_4.5 | all-reduce | flops 48 | bytes 384 | tf_op jit(solution)/shard_map/pmax | solution.py:74
  174.6 34.0 %all_to_all.24 = f32[16,1,3]{2,1,0:T(1,128)S(1)} all-to-all(f32[16,1,3]{2,1,0:T(1,128)S(1)} %bitcast.111), channel_id=1, replica_groups=mesh['cls'=16,'dir'=32] {'cls'}, dimensions={0} | all-to-all | bytes 384 | tf_op jit(solution)/shard_map/all_to_all | solution.py:75
  208.6 0.5 broadcast.40
  209.1 0.7 reduce.11
  209.9 0.8 multiply_reduce_fusion
  210.7 24.2 %psum.7 = f32[]{:T(128)} all-reduce(f32[]{:T(128)} %get-tuple-element.47), channel_id=1, replica_groups=mesh['cls'=16,'dir'=32] {'cls'}, use_global_device_ids=true, to_apply=%region_6.7 | all-reduce | flops 1 | bytes 8 | tf_op jit(solution)/shard_map/psum | solution.py:79
  235.6 0.5 broadcast_divide_fusion
  (54 shorter events, 9.4 us)
Async XLA Ops:
  0.6 27.7 %copy-start = (f32[64,33]{0,1:T(8,128)S(1)}, f32[64,33]{0,1:T(8,128)}, u32[]{:S(2)}) copy-start(f32[64,33]{0,1:T(8,128)} %param.8) | copy-start | bytes 25348
  4.4 18.8 %all-to-all-start.1 = ((bf16[16,1,3]{2,1,0:T(2,128)(2,1)}), bf16[16,1,3]{2,1,0:T(2,128)(2,1)S(1)}, u32[]{:S(2)}, u32[]{:S(2)}) async-start(bf16[16,1,3]{2,1,0:T(2,128)(2,1)} %all_to_all.20), calls=%async_computation.1 | async-start | bytes 16384 | tf_op jit(solution)/shard_map/all_to_all | solution.py:37
  23.3 12.2 %all-to-all-start = ((bf16[16,2,198]{2,1,0:T(2,128)(2,1)}), bf16[16,2,198]{2,1,0:T(2,128)(2,1)S(1)}, u32[]{:S(2)}, u32[]{:S(2)}) async-start(bf16[16,2,198]{2,1,0:T(2,128)(2,1)} %reshape.103), calls=%async_computation | async-start | bytes 32768 | tf_op jit(solution)/shard_map/all_to_all | solution.py:36
  97.1 1.8 copy-start.2
  97.1 1.8 copy-start.3
  100.1 4.2 %copy-start.1 = (bf16[48,33,8]{2,1,0:T(8,128)(2,1)S(1)}, bf16[48,33,8]{2,1,0:T(8,128)(2,1)}, u32[]{:S(2)}) copy-start(bf16[48,33,8]{2,1,0:T(8,128)(2,1)} %get-tuple-element.14) | copy-start | bytes 76036
  104.7 5.3 %copy-start.4 = (bf16[1,144,4224]{2,1,0:T(8,128)(2,1)S(1)}, bf16[1,144,4224]{2,1,0:T(8,128)(2,1)}, u32[]{:S(2)}) copy-start(bf16[1,144,4224]{2,1,0:T(8,128)(2,1)} %param.9) | copy-start | bytes 3649540
  210.7 25.4 %copy-start.5 = (f32[16]{0:T(128)}, f32[16]{0:T(128)S(1)}, u32[]{:S(2)}) copy-start(f32[16]{0:T(128)S(1)} %get-tuple-element.48) | copy-start | bytes 196
where the time goes:
time: 237 us; the launch traced here: 236 us
  blocking collectives  168 us (71%)
  local copies, waits for them, and re-layouts  21.9 us (9%)
  starting transfers between devices  16.7 us (7%)
  other arithmetic  10.8 us (5%)
  waiting for transfers between devices  8.61 us (4%)
  matrix products  8.15 us (3%)
    pmax x1, blocking collectives, on_device(): group_best = lax.pmax(local_best, 'dir')  59 us
    all_gather x1, blocking collectives, on_device(): panels = lax.all_gather(arrived, 'dir', axis=2, tiled=True)  51 us
    all_to_all x1, blocking collectives, on_device(): lax.all_to_all(group_best.reshape(classes, capacity), 'cls', split_axis=0...  34 us
    psum x1, blocking collectives, on_device(): spread = lax.psum(jnp.sum(own_best * own_best), 'cls')  24.2 us
    all_to_all x1, starting transfers between devices, on_device(): lax.all_to_all(bins_sent, 'cls', split_axis=0, concat_axis=0, tiled=True)  11.8 us
    all_to_all x1, waiting for transfers between devices, on_device(): lax.all_to_all(packed, 'cls', split_axis=0, concat_axis=0, tiled=True)  6.29 us
    unnamed x15, other arithmetic  5.67 us
    all_gather x1, local copies, waits for them, and re-layouts, on_device(): panels = lax.all_gather(arrived, 'dir', axis=2, tiled=True)  5.56 us
  transfers between devices with their start and end apart: 2, of which 2 were waited for; matrix products, arithmetic and copies ran while one was open for 2% of the time, Pallas kernels for 0%

commit v1 on v0

v1 whole, which is shorter than its diff:
```python
import math

import jax
import jax.numpy as jnp
from jax import lax
from jax.experimental import pallas as pl
from jax.experimental.pallas import tpu as pltpu
from jax.sharding import PartitionSpec as P

CYCLES = 33
ANGLES = 64
ROTS = 16
WIDE = 2 * ANGLES
FEAT = CYCLES * WIDE
STEP = 2 * (ANGLES // ROTS)
SCALE = 1.0 / math.sqrt(FEAT / 3.0)
NCLS = 16
NX = 4
NY = 8
NDIR = NX * NY
ROWS = 16
CAP = 3
SLOTS = NCLS * CAP
BINS = 64
TOTAL = 256
MESH = pl.DeviceIdType.MESH
HIGH = lax.Precision.HIGHEST
F32 = jnp.float32
BF16 = jnp.bfloat16
I32 = jnp.int32
HOPS = {1: (0, 1), 7: (0, 7), 2: (1, 0), 6: (3, 0), 3: (1, 1), 5: (3, 7), 4: (2, 0)}
ORDER = (1, 7, 2, 6, 3, 5, 4)


def iota(shape, dim):
    return lax.broadcasted_iota(I32, shape, dim)


def to_column(row, n):
    keep = iota((n, n), 0) == iota((n, n), 1)
    return jnp.sum(jnp.where(keep, jnp.broadcast_to(row, (n, n)), 0), axis=1, keepdims=True)


def to_row(column, n, lanes):
    keep = iota((n, lanes), 0) == iota((n, lanes), 1)
    return jnp.sum(
        jnp.where(keep, jnp.broadcast_to(column, (n, lanes)), 0), axis=0, keepdims=True
    )


def kernel(
    part_ref, assign_ref, bins_ref, table_ref, refs_ref, best_ref, norm_ref,
    tbuf, tset, tlast, energy, send0, send1, a0, a1, stack, bsend, brecv,
    gmain, gext, lhs, acc, dsend, dbuf, esend, ebuf,
    load_sem, a_send, a_recv, b_send, b_recv, c_send, c_recv, x_send, x_recv,
    d_send, d_recv, e_send, e_recv,
):
    me_c = lax.axis_index("cls")
    me_d = lax.axis_index("dir")
    x = lax.rem(me_d, NX)
    y = lax.div(me_d, NX)
    s = lax.rem(2 * x + y, 8)

    load = pltpu.make_async_copy(refs_ref.at[0], tbuf, load_sem)
    load.start()

    barrier = pltpu.get_barrier_semaphore()
    for d in range(1, NDIR):
        pl.semaphore_signal(
            barrier, inc=1, device_id=(me_c, lax.rem(me_d + d, NDIR)), device_id_type=MESH
        )
    for d in range(1, NCLS):
        pl.semaphore_signal(
            barrier, inc=1, device_id=(lax.rem(me_c + d, NCLS), me_d), device_id_type=MESH
        )

    assign_row = assign_ref[...]
    assign = to_column(assign_row, ROWS)
    bins = to_column(bins_ref[...], ROWS)
    same = (assign == jnp.broadcast_to(assign_row, (ROWS, ROWS))) & (
        iota((ROWS, ROWS), 1) < iota((ROWS, ROWS), 0)
    )
    placing = jnp.sum(same.astype(I32), axis=1, keepdims=True)
    slot = assign * CAP + placing

    onehot = bins == iota((ROWS, BINS), 1)
    row_a = table_ref[pl.ds(me_d, 1), :]
    row_b = table_ref[pl.ds(me_d + 1, 1), :]
    ctf_a = jnp.sum(jnp.where(onehot, row_a, 0.0), axis=1, keepdims=True)
    ctf_b = jnp.sum(jnp.where(onehot, row_b, 0.0), axis=1, keepdims=True)
    raw = jnp.concatenate(
        [part_ref[...].astype(F32), jnp.zeros((ROWS, 2 * WIDE - FEAT // NDIR), F32)], axis=1
    )
    raw = pltpu.roll(raw, 4 * me_d, 1)
    tile0 = (raw[:, :WIDE] * ctf_a).astype(BF16)
    tile1 = (raw[:, WIDE:] * ctf_b).astype(BF16)
    send0[...] = tile0
    send1[...] = tile1
    a0[x] = tile0

    lane = iota((ROWS, NCLS * ROWS), 1)
    to_class = lane // ROWS
    at_row = lane - to_class * ROWS
    third = (at_row * 171) >> 9
    hit = slot == to_class * CAP + at_row - third * CAP
    pieces = [(hit & (third == c)).astype(F32) for c in range(5)]
    pieces.append(((assign == to_class) & (at_row == ROWS - 1)).astype(F32))
    pieces.append(jnp.zeros((2 * ROWS, NCLS * ROWS), F32))
    packing = jnp.concatenate(pieces, axis=0).T.astype(BF16)
    aux = jnp.where(placing == iota((ROWS, WIDE), 1), (bins + 1).astype(F32), 0.0)
    stack[5 * ROWS : 6 * ROWS] = aux.astype(BF16)
    stack[6 * ROWS :] = jnp.zeros((2 * ROWS, WIDE), BF16)

    pl.semaphore_wait(barrier, NDIR + NCLS - 2)

    for d in range(1, NX):
        c = lax.rem(x + d, NX)
        to = lax.rem(s + 16 - 2 * c, NY) * NX + c
        pltpu.make_async_remote_copy(
            src_ref=send0, dst_ref=a0.at[x], send_sem=a_send, recv_sem=a_recv,
            device_id=(me_c, to), device_id_type=MESH,
        ).start()
    next_x = lax.rem(x + 1, NX)
    next_y = lax.rem(lax.div(me_d + 1, NX), NY)
    next_s = lax.rem(2 * next_x + next_y, 8)
    for c in range(NX):
        to = lax.rem(next_s + 16 - 2 * c, NY) * NX + c
        pltpu.make_async_remote_copy(
            src_ref=send1, dst_ref=a1.at[next_x], send_sem=a_send, recv_sem=a_recv,
            device_id=(me_c, to), device_id_type=MESH,
        ).start()

    q = iota((SLOTS, TOTAL), 0)
    sender = (q * 171) >> 9
    source = sender * ROWS + q - sender * CAP
    column = iota((SLOTS, TOTAL), 1)
    unpack = jnp.concatenate(
        [(column == source + c * CAP).astype(F32) for c in range(5)]
        + [(column == sender * ROWS + ROWS - 1).astype(F32)],
        axis=0,
    ).astype(BF16)

    a_all = stack.at[pl.ds(0, 7 * ROWS)]
    pltpu.make_async_copy(a_all, a_all, a_recv).wait()
    first = (s != 0).astype(F32)
    for c in range(NX):
        late = a1[c].astype(F32)
        if c == 0:
            stack[4 * ROWS : 5 * ROWS] = (late * (1.0 - first)).astype(BF16)
            late = late * first
        stack[c * ROWS : (c + 1) * ROWS] = (a0[c].astype(F32) + late).astype(BF16)

    packed = jnp.dot(packing, stack[...], preferred_element_type=F32)
    bsend[...] = packed.astype(BF16)
    mine = pl.ds(pl.multiple_of(me_c * ROWS, ROWS), ROWS)
    for d in range(1, NCLS):
        to = lax.rem(me_c + d, NCLS)
        pltpu.make_async_remote_copy(
            src_ref=bsend.at[pl.ds(pl.multiple_of(to * ROWS, ROWS), ROWS)],
            dst_ref=brecv.at[mine], send_sem=b_send, recv_sem=b_recv,
            device_id=(to, me_d), device_id_type=MESH,
        ).start()
    brecv[mine] = bsend[mine]

    load.wait()
    for c in range(NX):
        for z in range(8):
            j = ((z + 8 - 2 * c) % 8) * NX + c
            tset[z, :, c * WIDE : (c + 1) * WIDE] = tbuf[:, j * WIDE : (j + 1) * WIDE]
    tlast[...] = tbuf[:, (CYCLES - 1) * WIDE :]

    b_all = brecv.at[pl.ds(0, (NCLS - 1) * ROWS)]
    pltpu.make_async_copy(b_all, b_all, b_recv).wait()
    unpacked = jnp.dot(unpack, brecv[...], preferred_element_type=F32)
    gmain[0] = unpacked[: 4 * SLOTS].astype(BF16)

    @pl.when(s == 0)
    def _():
        gext[...] = unpacked[4 * SLOTS : 5 * SLOTS].astype(BF16)

    for d in ORDER:
        dx, dy = HOPS[d]
        to = lax.rem(y + dy, NY) * NX + lax.rem(x + dx, NX)
        pltpu.make_async_remote_copy(
            src_ref=gmain.at[0], dst_ref=gmain.at[d], send_sem=c_send, recv_sem=c_recv.at[d],
            device_id=(me_c, to), device_id_type=MESH,
        ).start()

    @pl.when(s == 0)
    def _():
        for d in ORDER:
            dx, dy = HOPS[d]
            to = lax.rem(y + dy, NY) * NX + lax.rem(x + dx, NX)
            pltpu.make_async_remote_copy(
                src_ref=gext, dst_ref=gext, send_sem=x_send, recv_sem=x_recv,
                device_id=(me_c, to), device_id_type=MESH,
            ).start()

    lanes = iota((1, WIDE), 1)
    total = jnp.zeros((tbuf.shape[0], WIDE), F32)
    for k in range(CYCLES):
        block = tbuf[:, k * WIDE : (k + 1) * WIDE].astype(F32)
        total = jnp.where(lanes == k, jnp.sum(block * block, axis=1, keepdims=True), total)
    energy[...] = total
    third_lane = iota((SLOTS, WIDE), 0) - 3 * ((iota((SLOTS, WIDE), 0) * 171) >> 9)
    got = jnp.sum(
        jnp.where(iota((SLOTS, WIDE), 1) == third_lane, unpacked[5 * SLOTS :], 0.0),
        axis=1, keepdims=True,
    ).astype(I32)
    bin_hot = (got == iota((SLOTS, BINS), 1) + 1).astype(F32)
    table = table_ref[...]
    table = jnp.concatenate([table, jnp.zeros((WIDE - CYCLES, BINS), F32)], axis=0)
    nt = (((1,), (1,)), ((), ()))
    ctf = lax.dot_general(bin_hot, table, nt, precision=HIGH, preferred_element_type=F32)
    penalty = 0.5 * lax.dot_general(
        ctf * ctf, energy[...], nt, precision=HIGH, preferred_element_type=F32
    )

    def turn(block, at):
        for r in range(ROTS):
            lhs[r * SLOTS : (r + 1) * SLOTS, at * WIDE : (at + 1) * WIDE] = pltpu.roll(
                block, r * STEP, 1
            )

    def add_set(d):
        for c in range(NX):
            turn(gmain[d, c * SLOTS : (c + 1) * SLOTS, :], c)
        term = lax.dot_general(
            lhs[...], tset[lax.rem(s + 8 - d, 8)], nt, preferred_element_type=F32
        )
        if d == 0:
            acc[...] = term
        else:
            acc[...] += term

    add_set(0)
    for d in ORDER:
        pltpu.make_async_copy(gmain.at[d], gmain.at[d], c_recv.at[d]).wait()
        add_set(d)

    @pl.when(s != 0)
    def _():
        pltpu.make_async_copy(gext, gext, x_recv).wait()

    turn(gext[...], 0)
    cross = acc[...] + lax.dot_general(
        lhs[:, :WIDE], tlast[...], nt, preferred_element_type=F32
    )
    top = cross[:SLOTS]
    for r in range(1, ROTS):
        top = jnp.maximum(top, cross[r * SLOTS : (r + 1) * SLOTS])
    local = jnp.max((top - penalty) * SCALE, axis=1, keepdims=True)
    local = to_row(local, SLOTS, WIDE)

    dsend[...] = local
    dbuf[me_d] = local
    for d in range(1, NDIR):
        pltpu.make_async_remote_copy(
            src_ref=dsend, dst_ref=dbuf.at[me_d], send_sem=d_send, recv_sem=d_recv,
            device_id=(me_c, lax.rem(me_d + d, NDIR)), device_id_type=MESH,
        ).start()
    d_all = dbuf.at[pl.ds(0, NDIR - 1)]
    pltpu.make_async_copy(d_all, d_all, d_recv).wait()
    group = jnp.max(dbuf[...], axis=0)

    squares = jnp.sum(group * group, axis=1, keepdims=True)
    answer = jnp.where(lanes == SLOTS, squares, group)
    esend[...] = answer
    ebuf[me_c] = answer
    for d in range(1, NCLS):
        pltpu.make_async_remote_copy(
            src_ref=esend, dst_ref=ebuf.at[me_c], send_sem=e_send, recv_sem=e_recv,
            device_id=(lax.rem(me_c + d, NCLS), me_d), device_id_type=MESH,
        ).start()
    e_all = ebuf.at[pl.ds(0, NCLS - 1)]
    pltpu.make_async_copy(e_all, e_all, e_recv).wait()

    spread = jnp.zeros((1, WIDE), F32)
    chosen = jnp.zeros((ROWS, WIDE), F32)
    for g in range(NCLS):
        spread = spread + ebuf[g]
        chosen = jnp.where(assign == g, ebuf[g], chosen)
    spread = jnp.sum(jnp.where(lanes == SLOTS, spread, 0.0), axis=1, keepdims=True)
    own = jnp.sum(
        jnp.where(iota((ROWS, WIDE), 1) == me_c * CAP + placing, chosen, 0.0),
        axis=1, keepdims=True,
    )
    own = to_row(own, ROWS, ROWS)
    best_ref[...] = own
    norm_ref[...] = own / jnp.sqrt(spread / TOTAL + 1e-05)

    a_all = stack.at[pl.ds(0, 7 * ROWS)]
    pltpu.make_async_copy(a_all, a_all, a_send).wait()
    pltpu.make_async_copy(b_all, b_all, b_send).wait()
    c_all = gmain.at[pl.ds(1, 7)]
    pltpu.make_async_copy(c_all, c_all, c_send).wait()

    @pl.when(s == 0)
    def _():
        x_all = lhs.at[pl.ds(0, 7 * SLOTS), pl.ds(0, WIDE)]
        pltpu.make_async_copy(x_all, x_all, x_send).wait()

    pltpu.make_async_copy(d_all, d_all, d_send).wait()
    pltpu.make_async_copy(e_all, e_all, e_send).wait()


def on_device(particles, assignments, defocus_bins, ctf_table, references):
    dirs = references.shape[1]
    vmem = pl.BlockSpec(memory_space=pltpu.VMEM)
    scratch = [
        pltpu.VMEM((dirs, FEAT), BF16),
        pltpu.VMEM((8, dirs, NX * WIDE), BF16),
        pltpu.VMEM((dirs, WIDE), BF16),
        pltpu.VMEM((dirs, WIDE), F32),
        pltpu.VMEM((ROWS, WIDE), BF16),
        pltpu.VMEM((ROWS, WIDE), BF16),
        pltpu.VMEM((NX, ROWS, WIDE), BF16),
        pltpu.VMEM((NX, ROWS, WIDE), BF16),
        pltpu.VMEM((8 * ROWS, WIDE), BF16),
        pltpu.VMEM((NCLS * ROWS, WIDE), BF16),
        pltpu.VMEM((NCLS * ROWS, WIDE), BF16),
        pltpu.VMEM((8, 4 * SLOTS, WIDE), BF16),
        pltpu.VMEM((SLOTS, WIDE), BF16),
        pltpu.VMEM((ROTS * SLOTS, NX * WIDE), BF16),
        pltpu.VMEM((ROTS * SLOTS, dirs), F32),
        pltpu.VMEM((1, WIDE), F32),
        pltpu.VMEM((NDIR, 1, WIDE), F32),
        pltpu.VMEM((1, WIDE), F32),
        pltpu.VMEM((NCLS, 1, WIDE), F32),
    ]
    dma = pltpu.SemaphoreType.DMA
    sems = [dma, dma, dma, dma, dma, dma, dma((8,)), dma, dma, dma, dma, dma, dma]
    best, norm = pl.pallas_call(
        kernel,
        out_shape=[jax.ShapeDtypeStruct((1, ROWS), F32)] * 2,
        in_specs=[vmem, vmem, vmem, vmem, pl.BlockSpec(memory_space=pl.ANY)],
        out_specs=[vmem, vmem],
        scratch_shapes=scratch + sems,
        compiler_params=pltpu.CompilerParams(
            collective_id=0, has_side_effects=True, vmem_limit_bytes=40 * 1024 * 1024
        ),
    )(
        particles,
        assignments.reshape(1, ROWS),
        defocus_bins.reshape(1, ROWS),
        ctf_table.T,
        references,
    )
    return best.reshape(ROWS), norm.reshape(ROWS)


def solution(mesh):
    placed = (P("cls", "dir"), P("cls", None), P("cls"), P(), P("cls", "dir", None))
    return jax.shard_map(
        on_device, mesh=mesh, in_specs=placed, out_specs=(P("cls"), P("cls")), check_vma=False
    )
```

time: 237 us -> 51.9 us (0.22)
  blocking collectives: 168 us -> 0 us
  Pallas kernels: 0 us -> 45.9 us
  local copies, waits for them, and re-layouts: 21.9 us -> 5.03 us
  starting transfers between devices: 16.7 us -> 0 us
  other arithmetic: 10.8 us -> 0 us
  waiting for transfers between devices: 8.61 us -> 0 us
  matrix products: 8.15 us -> 0 us
    pmax x1 -> x0, blocking collectives: 59 us -> none  [on_device(): group_best = lax.pmax(local_best, 'dir')]
    all_gather x1 -> x0, blocking collectives: 51 us -> none  [on_device(): panels = lax.all_gather(arrived, 'dir', axis=2, tiled=True)]
    pallas_call x0 -> x1, Pallas kernels: none -> 45.9 us  [on_device(): pl.pallas_call(kernel, out_shape=[jax.ShapeDtypeStruct((1, ROWS), F32)] *...]
    all_to_all x1 -> x0, blocking collectives: 34 us -> none  [on_device(): lax.all_to_all(group_best.reshape(classes, capacity), 'cls', split_axis=0...]
    psum x1 -> x0, blocking collectives: 24.2 us -> none  [on_device(): spread = lax.psum(jnp.sum(own_best * own_best), 'cls')]
    all_to_all x2 -> x0, starting transfers between devices: 16.7 us -> none  [the longest x1 11.8 us: on_device(): lax.all_to_all(bins_sent, 'cls', split_axis=0, concat_axis=0, tiled=True)]
    all_to_all x2 -> x0, waiting for transfers between devices: 8.61 us -> none  [the longest x1 6.29 us: on_device(): lax.all_to_all(packed, 'cls', split_axis=0, concat_axis=0, tiled=True)]
    dot_general x6 -> x0, matrix products: 8.15 us -> none  [the longest x1 5.24 us: block_best(): lax.dot_general(templates, turned, (((1,), (1,)), ((), ())), preferred_el...]
  transfers between devices with their start and end apart: 2 -> 0, of which waited for: 2 -> 0; matrix products, arithmetic and copies ran while one was open for 2% -> 0% of each run, Pallas kernels for 0% -> 0%
where the time goes in v1:
time: 51.9 us; the launch traced here: 51.6 us
  Pallas kernels  45.9 us (88%)
  local copies, waits for them, and re-layouts  5.03 us (10%)
  between operations  0.65 us (1%)
    pallas_call x1, Pallas kernels, on_device(): pl.pallas_call(kernel, out_shape=[jax.ShapeDtypeStruct((1, ROWS), F32)] *...  45.9 us
    unnamed x12, local copies, waits for them, and re-layouts  5.03 us

profile of v1, /device:TPU:1, one launch (start us, length us, event | category | flops | bytes accessed | tf_op | source)
XLA Modules:
  0.0 51.6 jit_solution(17053561423999307210)
XLA Ops:
  0.6 0.0 copy-start
  0.6 1.3 %copy-done = bf16[1,144,4224]{2,1,0:T(8,128)(2,1)S(1)} copy-done((bf16[1,144,4224]{2,1,0:T(8,128)(2,1)S(1)}, bf16[1,144,4224]{2,1,0:T(8,128)(2,1)}, u32[]{:S(2)}) %copy-start) | copy-done | bytes 1216536
  1.9 0.0 copy-start.1
  1.9 0.7 %copy-done.1 = f32[64,33]{0,1:T(8,128)S(1)} copy-done((f32[64,33]{0,1:T(8,128)S(1)}, f32[64,33]{0,1:T(8,128)}, u32[]{:S(2)}) %copy-start.1) | copy-done | bytes 8472
  2.6 0.0 copy-start.2
  2.6 0.7 %copy-done.2 = bf16[16,132]{1,0:T(8,128)(2,1)S(1)} copy-done((bf16[16,132]{1,0:T(8,128)(2,1)S(1)}, bf16[16,132]{1,0:T(8,128)(2,1)}, u32[]{:S(2)}) %copy-start.2) | copy-done | bytes 4248
  3.3 0.0 copy-start.3
  3.3 0.7 %copy-done.3 = s32[16,1]{0,1:T(1,128)S(1)} copy-done((s32[16,1]{0,1:T(1,128)S(1)}, s32[16,1]{0,1:T(1,128)}, u32[]{:S(2)}) %copy-start.3) | copy-done | bytes 88
  4.0 0.0 copy-start.4
  4.0 0.7 %copy-done.4 = s32[16]{0:T(128)S(1)} copy-done((s32[16]{0:T(128)S(1)}, s32[16]{0:T(128)}, u32[]{:S(2)}) %copy-start.4) | copy-done | bytes 88
  4.7 45.9 %shard_map.68 = (f32[1,16]{1,0:T(1,128)S(1)}, f32[1,16]{1,0:T(1,128)S(1)}) custom-call(bf16[16,132]{1,0:T(8,128)(2,1)S(1)} %copy-done.2, s32[1,16]{1,0:T(1,128)S(1)} %bitcast.6, s32[1,16]{1,0:T(1,128)S(1)} %bitcast.7, f32[33,64]{1,0:T(8,128)S(1)} %bitcast.5, bf16[1,144,4224]{2,1,0:T(8,128)(2,1)S(1)} %copy-done), custom_call_target="tpu_custom_call" | custom-call | tf_op jit(solution)/shard_map/pallas_call | solution.py:333
  50.6 0.5 copy.9
  51.1 0.5 copy.10
Async XLA Ops:
  0.6 1.3 %copy-start = (bf16[1,144,4224]{2,1,0:T(8,128)(2,1)S(1)}, bf16[1,144,4224]{2,1,0:T(8,128)(2,1)}, u32[]{:S(2)}) copy-start(bf16[1,144,4224]{2,1,0:T(8,128)(2,1)} %refs_ref.1) | copy-start | bytes 3649540
  1.9 0.7 %copy-start.1 = (f32[64,33]{0,1:T(8,128)S(1)}, f32[64,33]{0,1:T(8,128)}, u32[]{:S(2)}) copy-start(f32[64,33]{0,1:T(8,128)} %param.8) | copy-start | bytes 25348
  2.6 0.7 %copy-start.2 = (bf16[16,132]{1,0:T(8,128)(2,1)S(1)}, bf16[16,132]{1,0:T(8,128)(2,1)}, u32[]{:S(2)}) copy-start(bf16[16,132]{1,0:T(8,128)(2,1)} %part_ref.1) | copy-start | bytes 12676
  3.3 0.7 %copy-start.3 = (s32[16,1]{0,1:T(1,128)S(1)}, s32[16,1]{0,1:T(1,128)}, u32[]{:S(2)}) copy-start(s32[16,1]{0,1:T(1,128)} %param.6) | copy-start | bytes 196
  4.0 0.7 %copy-start.4 = (s32[16]{0:T(128)S(1)}, s32[16]{0:T(128)}, u32[]{:S(2)}) copy-start(s32[16]{0:T(128)} %param.7) | copy-start | bytes 196

commit v2 on v1

v2 whole, which is shorter than its diff:
```python
import math

import jax
import jax.numpy as jnp
from jax import lax
from jax.experimental import pallas as pl
from jax.experimental.pallas import tpu as pltpu
from jax.sharding import PartitionSpec as P

CYCLES = 33
ANGLES = 64
ROTS = 16
WIDE = 2 * ANGLES
FEAT = CYCLES * WIDE
STEP = 2 * (ANGLES // ROTS)
SCALE = 1.0 / math.sqrt(FEAT / 3.0)
NCLS = 16
NX = 4
NY = 8
NDIR = NX * NY
ROWS = 16
CAP = 3
SLOTS = NCLS * CAP
BINS = 64
TOTAL = 256
MESH = pl.DeviceIdType.MESH
HIGH = lax.Precision.HIGHEST
F32 = jnp.float32
BF16 = jnp.bfloat16
I32 = jnp.int32
LIMIT = 63 * 1024 * 1024


def iota(shape, dim):
    return lax.broadcasted_iota(I32, shape, dim)


def to_column(row, n):
    keep = iota((n, n), 0) == iota((n, n), 1)
    return jnp.sum(jnp.where(keep, jnp.broadcast_to(row, (n, n)), 0), axis=1, keepdims=True)


def to_row(column, n, lanes):
    keep = iota((n, lanes), 0) == iota((n, lanes), 1)
    return jnp.sum(
        jnp.where(keep, jnp.broadcast_to(column, (n, lanes)), 0), axis=0, keepdims=True
    )


def settle(ref, sem):
    pltpu.make_async_copy(ref, ref, sem).wait()


def kernel(
    part_hbm, assign_hbm, bins_hbm, table_hbm, refs_hbm, out_ref,
    part_ref, assign_ref, bins_ref, table_ref, tbuf, energy, bsend, brecv,
    grid, aux4, lhs, acc, dsend, dbuf, esend, ebuf,
    in_sem, load_sem, b_send, b_recv, y_send, y_recv, x_send, x_recv, u_send, u_recv,
    d_send, d_recv, e_send, e_recv,
):
    me_c = lax.axis_index("cls")
    me_d = lax.axis_index("dir")
    x = lax.rem(me_d, NX)
    y = lax.div(me_d, NX)

    barrier = pltpu.get_barrier_semaphore()
    peers = [(lax.rem(me_c + d, NCLS), me_d) for d in range(1, NCLS)]
    peers += [(me_c, lax.rem(y + d, NY) * NX + x) for d in range(1, NY)]
    peers += [(me_c, y * NX + lax.rem(x + d, NX)) for d in range(1, NX)]
    for peer in peers:
        pl.semaphore_signal(barrier, inc=1, device_id=peer, device_id_type=MESH)
    inputs = [
        pltpu.make_async_copy(source, target, in_sem.at[n])
        for n, (source, target) in enumerate(
            [
                (assign_hbm, assign_ref),
                (bins_hbm, bins_ref),
                (table_hbm, table_ref),
                (part_hbm, part_ref),
            ]
        )
    ]
    for copy in inputs:
        copy.start()
    load = pltpu.make_async_copy(refs_hbm.at[0], tbuf, load_sem)
    load.start()

    q = iota((4 * ROWS, TOTAL), 0)
    unpack = (iota((4 * ROWS, TOTAL), 1) == (q & 15) * ROWS + (q >> 4)).astype(F32).astype(BF16)
    for copy in inputs:
        copy.wait()

    assign_row = assign_ref[...]
    assign = to_column(assign_row, ROWS)
    bins = to_column(bins_ref[...], ROWS)
    same = (assign == jnp.broadcast_to(assign_row, (ROWS, ROWS))) & (
        iota((ROWS, ROWS), 1) < iota((ROWS, ROWS), 0)
    )
    placing = jnp.sum(same.astype(I32), axis=1, keepdims=True)

    lane = iota((ROWS, NCLS * ROWS), 1)
    at_row = lane & (ROWS - 1)
    named = assign == lane >> 4
    packing = jnp.concatenate(
        [
            (named & (at_row == placing)).astype(F32),
            (named & (at_row == CAP)).astype(F32),
            jnp.zeros((6 * ROWS, NCLS * ROWS), F32),
        ],
        axis=0,
    ).T.astype(BF16)

    onehot = bins == iota((ROWS, BINS), 1)
    row_a = table_ref[pl.ds(me_d, 1), :]
    row_b = table_ref[pl.ds(me_d + 1, 1), :]
    ctf_a = jnp.sum(jnp.where(onehot, row_a, 0.0), axis=1, keepdims=True)
    ctf_b = jnp.sum(jnp.where(onehot, row_b, 0.0), axis=1, keepdims=True)
    raw = part_ref[...].astype(F32)
    wide = iota((ROWS, WIDE), 1)
    main = raw[:, :WIDE]
    main = main * jnp.where(wide < WIDE - 4 * me_d, ctf_a, ctf_b)
    main = pltpu.roll(main, 4 * me_d, 1)
    left = jnp.concatenate([raw[:, WIDE:], jnp.zeros((ROWS, WIDE - 4), F32)], axis=1) * ctf_b
    aux = jnp.where(wide == 96 + placing, (bins + 1).astype(F32), 0.0)
    for t in range(CAP):
        aux = aux + jnp.where(placing == t, pltpu.roll(left, 12 * y + 4 * t, 1), 0.0)
    stack = jnp.concatenate([main, aux, jnp.zeros((6 * ROWS, WIDE), F32)], axis=0).astype(BF16)
    bsend[...] = jnp.dot(packing, stack, preferred_element_type=F32).astype(BF16)
    mine = pl.ds(pl.multiple_of(me_c * ROWS, ROWS), ROWS)
    brecv[mine] = bsend[mine]

    pl.semaphore_wait(barrier, len(peers))

    for d in (8, 9, 7, 10, 6, 11, 5, 12, 4, 13, 3, 14, 2, 15, 1):
        to = lax.rem(me_c + d, NCLS)
        pltpu.make_async_remote_copy(
            src_ref=bsend.at[pl.ds(pl.multiple_of(to * ROWS, ROWS), ROWS)],
            dst_ref=brecv.at[mine], send_sem=b_send, recv_sem=b_recv,
            device_id=(to, me_d), device_id_type=MESH,
        ).start()

    load.wait()
    lanes = iota((1, WIDE), 1)
    total = jnp.zeros((tbuf.shape[0], WIDE), F32)
    for k in range(CYCLES):
        block = tbuf[:, k * WIDE : (k + 1) * WIDE].astype(F32)
        total = jnp.where(lanes == k, jnp.sum(block * block, axis=1, keepdims=True), total)
    energy[...] = total

    b_all = brecv.at[pl.ds(0, (NCLS - 1) * ROWS)]
    settle(b_all, b_recv)
    unpacked = jnp.dot(unpack, brecv[...], preferred_element_type=F32)
    own = grid.at[y, x]
    own[...] = unpacked.astype(BF16)

    def forward(rho):
        row = lax.rem(y + rho, NY)
        block = grid.at[row, x, pl.ds(0, SLOTS)]
        for d in (2, 1, 3):
            pltpu.make_async_remote_copy(
                src_ref=block, dst_ref=block, send_sem=x_send, recv_sem=x_recv.at[d, rho],
                device_id=(me_c, y * NX + lax.rem(x + d, NX)), device_id_type=MESH,
            ).start()

    for d in (4, 3, 5, 2, 6, 1, 7):
        pltpu.make_async_remote_copy(
            src_ref=own, dst_ref=own, send_sem=y_send, recv_sem=y_recv.at[NY - d],
            device_id=(me_c, lax.rem(y + d, NY) * NX + x), device_id_type=MESH,
        ).start()
    forward(0)

    nt = (((1,), (1,)), ((), ()))
    got = jnp.concatenate(
        [unpacked[SLOTS:, 96 + t : 97 + t] for t in range(CAP)], axis=0
    ).astype(I32)
    bin_hot = (got == iota((SLOTS, BINS), 1) + 1).astype(F32)
    table = jnp.concatenate([table_ref[...], jnp.zeros((WIDE - CYCLES, BINS), F32)], axis=0)
    ctf = lax.dot_general(bin_hot, table, nt, precision=HIGH, preferred_element_type=F32)
    penalty = 0.5 * lax.dot_general(
        ctf * ctf, energy[...], nt, precision=HIGH, preferred_element_type=F32
    )

    for rho in (1, 7, 2, 6, 3, 5, 4):
        settle(grid.at[0, 0], y_recv.at[rho])
        forward(rho)
    over = jnp.zeros((ROWS, WIDE), F32)
    for row in range(NY):
        over = over + grid[row, x, SLOTS:, :].astype(F32)
    aux4[x] = over.astype(BF16)
    for d in (2, 1, 3):
        pltpu.make_async_remote_copy(
            src_ref=aux4.at[x], dst_ref=aux4.at[x], send_sem=u_send, recv_sem=u_recv,
            device_id=(me_c, y * NX + lax.rem(x + d, NX)), device_id_type=MESH,
        ).start()

    at = iota((1, CAP * WIDE), 1)
    place, at = at >> 7, at & (WIDE - 1)
    spread_to = ((at >> 2) & 3) * WIDE + (at >> 4) * 12 + place * 4 + (at & 3)
    spreading = (iota((NX * WIDE, CAP * WIDE), 0) == spread_to).astype(F32).astype(BF16)

    for rho in (0, 1, 7, 2, 6, 3, 5, 4):
        for d in range(1, NX):
            settle(grid.at[0, 0, pl.ds(0, SLOTS)], x_recv.at[d, rho])
    settle(aux4.at[pl.ds(0, 3)], u_recv)

    rest = jnp.concatenate([aux4[c] for c in range(NX)], axis=1)
    rest = jnp.dot(rest, spreading, preferred_element_type=F32).astype(BF16)
    rest = jnp.concatenate([rest[:, t * WIDE : (t + 1) * WIDE] for t in range(CAP)], axis=0)

    def turn(block, at):
        for r in range(ROTS):
            lhs[r * SLOTS : (r + 1) * SLOTS, at * WIDE : (at + 1) * WIDE] = pltpu.roll(
                block, r * STEP, 1
            )

    def select(low, high):
        return ((lanes >= low) & (lanes < high)).astype(F32).astype(BF16)

    def cycle(k):
        block = None
        if k < NDIR:
            block = grid[k // NX, k % NX, :SLOTS, :] * select(4 * k, WIDE)
        if k > 0:
            j = k - 1
            early = grid[j // NX, j % NX, :SLOTS, :] * select(0, 4 * j)
            early = early + rest * select(4 * j, 4 * k)
            block = early if block is None else block + early
        return block

    for row in range(NY):
        for c in range(NX):
            turn(cycle(row * NX + c), c)
        term = lax.dot_general(
            lhs[...], tbuf[:, row * NX * WIDE : (row + 1) * NX * WIDE], nt,
            preferred_element_type=F32,
        )
        if row == 0:
            acc[...] = term
        else:
            acc[...] += term
    turn(cycle(NDIR), 0)
    cross = acc[...] + lax.dot_general(
        lhs[:, :WIDE], tbuf[:, NDIR * WIDE :], nt, preferred_element_type=F32
    )
    top = cross[:SLOTS]
    for r in range(1, ROTS):
        top = jnp.maximum(top, cross[r * SLOTS : (r + 1) * SLOTS])
    local = jnp.max((top - penalty) * SCALE, axis=1, keepdims=True)
    local = to_row(local, SLOTS, WIDE)

    dsend[...] = local
    dbuf[me_d] = local
    far = sorted(range(1, NDIR), key=lambda d: -min(d // NX, NY - d // NX))
    for d in far:
        pltpu.make_async_remote_copy(
            src_ref=dsend, dst_ref=dbuf.at[me_d], send_sem=d_send, recv_sem=d_recv,
            device_id=(me_c, lax.rem(me_d + d, NDIR)), device_id_type=MESH,
        ).start()
    d_all = dbuf.at[pl.ds(0, NDIR - 1)]
    settle(d_all, d_recv)
    group = jnp.max(dbuf[...], axis=0)

    squares = jnp.sum(group * group, axis=1, keepdims=True)
    answer = jnp.where(lanes == SLOTS, squares, group)
    esend[...] = answer
    ebuf[me_c] = answer
    for d in (8, 9, 7, 10, 6, 11, 5, 12, 4, 13, 3, 14, 2, 15, 1):
        pltpu.make_async_remote_copy(
            src_ref=esend, dst_ref=ebuf.at[me_c], send_sem=e_send, recv_sem=e_recv,
            device_id=(lax.rem(me_c + d, NCLS), me_d), device_id_type=MESH,
        ).start()
    settle(b_all, b_send)
    settle(grid.at[pl.ds(0, 7), 0], y_send)
    settle(grid.at[pl.ds(0, NY), pl.ds(0, 3), pl.ds(0, SLOTS)], x_send)
    settle(aux4.at[pl.ds(0, 3)], u_send)
    settle(d_all, d_send)

    e_all = ebuf.at[pl.ds(0, NCLS - 1)]
    settle(e_all, e_recv)
    spread = jnp.zeros((1, WIDE), F32)
    chosen = jnp.zeros((ROWS, WIDE), F32)
    for g in range(NCLS):
        spread = spread + ebuf[g]
        chosen = jnp.where(assign == g, ebuf[g], chosen)
    spread = jnp.sum(jnp.where(lanes == SLOTS, spread, 0.0), axis=1, keepdims=True)
    best = jnp.sum(
        jnp.where(wide == placing * ROWS + me_c, chosen, 0.0), axis=1, keepdims=True
    )
    best = to_row(best, ROWS, ROWS)
    out_ref[0:1, :] = best
    out_ref[1:2, :] = best / jnp.sqrt(spread / TOTAL + 1e-05)
    settle(e_all, e_send)


def on_device(particles, assignments, defocus_bins, ctf_table, references):
    dirs = references.shape[1]
    vmem = pl.BlockSpec(memory_space=pltpu.VMEM)
    scratch = [
        pltpu.VMEM((ROWS, FEAT // NDIR), BF16),
        pltpu.VMEM((1, ROWS), I32),
        pltpu.VMEM((1, ROWS), I32),
        pltpu.VMEM((CYCLES, BINS), F32),
        pltpu.VMEM((dirs, FEAT), BF16),
        pltpu.VMEM((dirs, WIDE), F32),
        pltpu.VMEM((NCLS * ROWS, WIDE), BF16),
        pltpu.VMEM((NCLS * ROWS, WIDE), BF16),
        pltpu.VMEM((NY, NX, 4 * ROWS, WIDE), BF16),
        pltpu.VMEM((NX, ROWS, WIDE), BF16),
        pltpu.VMEM((ROTS * SLOTS, NX * WIDE), BF16),
        pltpu.VMEM((ROTS * SLOTS, dirs), F32),
        pltpu.VMEM((1, WIDE), F32),
        pltpu.VMEM((NDIR, 1, WIDE), F32),
        pltpu.VMEM((1, WIDE), F32),
        pltpu.VMEM((NCLS, 1, WIDE), F32),
    ]
    dma = pltpu.SemaphoreType.DMA
    sems = [dma((4,)), dma, dma, dma, dma, dma((NY,)), dma, dma((NX, NY))] + [dma] * 6
    out = pl.pallas_call(
        kernel,
        out_shape=jax.ShapeDtypeStruct((2, ROWS), F32),
        in_specs=[pl.BlockSpec(memory_space=pl.ANY)] * 5,
        out_specs=vmem,
        scratch_shapes=scratch + sems,
        compiler_params=pltpu.CompilerParams(
            collective_id=0, has_side_effects=True, vmem_limit_bytes=LIMIT
        ),
    )(
        particles,
        assignments.reshape(1, ROWS),
        defocus_bins.reshape(1, ROWS),
        ctf_table.T,
        references,
    )
    return out[0], out[1]


def solution(mesh):
    placed = (P("cls", "dir"), P("cls", None), P("cls"), P(), P("cls", "dir", None))
    return jax.shard_map(
        on_device, mesh=mesh, in_specs=placed, out_specs=(P("cls"), P("cls")), check_vma=False
    )
```

time: 51.9 us -> 46.2 us (0.89)
  local copies, waits for them, and re-layouts: 5.03 us -> 1.25 us
  Pallas kernels: 45.9 us -> 44.2 us
    unnamed x12 -> x0, local copies, waits for them, and re-layouts: 5.03 us -> none
    pallas_call x1, Pallas kernels: 45.9 us -> 44.2 us  [on_device(): pl.pallas_call(kernel, out_shape=jax.ShapeDtypeStruct((2, ROWS), F32), in...]
    squeeze x0 -> x1, local copies, waits for them, and re-layouts: none -> 1.25 us  [on_device(): return (out[0], out[1])]
where the time goes in v2:
time: 46.2 us; the launch traced here: 46.1 us
  Pallas kernels  44.2 us (96%)
  local copies, waits for them, and re-layouts  1.25 us (3%)
  between operations  0.64 us (1%)
    pallas_call x1, Pallas kernels, on_device(): pl.pallas_call(kernel, out_shape=jax.ShapeDtypeStruct((2, ROWS), F32), in...  44.2 us
    squeeze x1, local copies, waits for them, and re-layouts, on_device(): return (out[0], out[1])  1.25 us

profile of v2, /device:TPU:1, one launch (start us, length us, event | category | flops | bytes accessed | tf_op | source)
XLA Modules:
  0.0 46.1 jit_solution(6743193479497790859)
XLA Ops:
  0.6 44.2 %shard_map.68 = f32[2,16]{1,0:T(2,128)} custom-call(bf16[16,132]{1,0:T(8,128)(2,1)} %part_hbm.1, s32[1,16]{1,0:T(1,128)} %bitcast.8, s32[1,16]{1,0:T(1,128)} %bitcast.9, f32[33,64]{1,0:T(8,128)} %bitcast.7, bf16[1,144,4224]{2,1,0:T(8,128)(2,1)} %refs_hbm.1), custom_call_target="tpu_custom_call" | custom-call | tf_op jit(solution)/shard_map/pallas_call | solution.py:318
  44.8 1.3 %slice_bitcast_fusion = (f32[16]{0:T(128)}, f32[16]{0:T(128)}) fusion(f32[2,16]{1,0:T(2,128)} %shard_map.68), kind=kLoop, calls=%fused_computation | loop fusion | bytes 256 | tf_op jit(solution)/shard_map/squeeze | solution.py:334

commit v3 on v2

--- a/solution.py
+++ b/solution.py
@@ -22,6 +22,8 @@
 CAP = 3
 SLOTS = NCLS * CAP
 BINS = 64
+HALF = ROTS // 2
+OUTWARD = (8, 9, 7, 10, 6, 11, 5, 12, 4, 13, 3, 14, 2, 15, 1)
 TOTAL = 256
 MESH = pl.DeviceIdType.MESH
 HIGH = lax.Precision.HIGHEST
@@ -64,7 +66,7 @@
     y = lax.div(me_d, NX)
 
     barrier = pltpu.get_barrier_semaphore()
-    peers = [(lax.rem(me_c + d, NCLS), me_d) for d in range(1, NCLS)]
+    peers = [(lax.rem(me_c + d, NCLS), me_d) for d in OUTWARD]
     peers += [(me_c, lax.rem(y + d, NY) * NX + x) for d in range(1, NY)]
     peers += [(me_c, y * NX + lax.rem(x + d, NX)) for d in range(1, NX)]
     for peer in peers:
@@ -82,7 +84,8 @@
     ]
     for copy in inputs:
         copy.start()
-    load = pltpu.make_async_copy(refs_hbm.at[0], tbuf, load_sem)
+    dirs = refs_hbm.shape[1]
+    load = pltpu.make_async_copy(refs_hbm.at[0], tbuf.at[pl.ds(0, dirs)], load_sem)
     load.start()
 
     q = iota((4 * ROWS, TOTAL), 0)
@@ -93,22 +96,15 @@
     assign_row = assign_ref[...]
     assign = to_column(assign_row, ROWS)
     bins = to_column(bins_ref[...], ROWS)
-    same = (assign == jnp.broadcast_to(assign_row, (ROWS, ROWS))) & (
-        iota((ROWS, ROWS), 1) < iota((ROWS, ROWS), 0)
-    )
-    placing = jnp.sum(same.astype(I32), axis=1, keepdims=True)
-
-    lane = iota((ROWS, NCLS * ROWS), 1)
-    at_row = lane & (ROWS - 1)
-    named = assign == lane >> 4
-    packing = jnp.concatenate(
-        [
-            (named & (at_row == placing)).astype(F32),
-            (named & (at_row == CAP)).astype(F32),
-            jnp.zeros((6 * ROWS, NCLS * ROWS), F32),
-        ],
-        axis=0,
-    ).T.astype(BF16)
+    together = assign == jnp.broadcast_to(assign_row, (ROWS, ROWS))
+    down, across = iota((ROWS, ROWS), 0), iota((ROWS, ROWS), 1)
+    placing = jnp.sum((together & (across < down)).astype(I32), axis=1, keepdims=True)
+    placing_row = jnp.sum((together & (down < across)).astype(I32), axis=0, keepdims=True)
+
+    at = iota((NCLS * ROWS, ROWS), 0)
+    named = assign_row == at >> 4
+    pack_main = (named & ((at & (ROWS - 1)) == placing_row)).astype(F32).astype(BF16)
+    pack_aux = (named & ((at & (ROWS - 1)) == CAP)).astype(F32).astype(BF16)
 
     onehot = bins == iota((ROWS, BINS), 1)
     row_a = table_ref[pl.ds(me_d, 1), :]
@@ -124,14 +120,16 @@
     aux = jnp.where(wide == 96 + placing, (bins + 1).astype(F32), 0.0)
     for t in range(CAP):
         aux = aux + jnp.where(placing == t, pltpu.roll(left, 12 * y + 4 * t, 1), 0.0)
-    stack = jnp.concatenate([main, aux, jnp.zeros((6 * ROWS, WIDE), F32)], axis=0).astype(BF16)
-    bsend[...] = jnp.dot(packing, stack, preferred_element_type=F32).astype(BF16)
+    bsend[...] = (
+        jnp.dot(pack_main, main.astype(BF16), preferred_element_type=F32)
+        + jnp.dot(pack_aux, aux.astype(BF16), preferred_element_type=F32)
+    ).astype(BF16)
     mine = pl.ds(pl.multiple_of(me_c * ROWS, ROWS), ROWS)
     brecv[mine] = bsend[mine]
 
     pl.semaphore_wait(barrier, len(peers))
 
-    for d in (8, 9, 7, 10, 6, 11, 5, 12, 4, 13, 3, 14, 2, 15, 1):
+    for d in OUTWARD:
         to = lax.rem(me_c + d, NCLS)
         pltpu.make_async_remote_copy(
             src_ref=bsend.at[pl.ds(pl.multiple_of(to * ROWS, ROWS), ROWS)],
@@ -141,9 +139,11 @@
 
     load.wait()
     lanes = iota((1, WIDE), 1)
-    total = jnp.zeros((tbuf.shape[0], WIDE), F32)
+    total = jnp.zeros((dirs, WIDE), F32)
     for k in range(CYCLES):
-        block = tbuf[:, k * WIDE : (k + 1) * WIDE].astype(F32)
+        block = tbuf[:dirs, k * WIDE : (k + 1) * WIDE]
+        tbuf[dirs:, k * WIDE : (k + 1) * WIDE] = pltpu.roll(block, WIDE // 2, 1)
+        block = block.astype(F32)
         total = jnp.where(lanes == k, jnp.sum(block * block, axis=1, keepdims=True), total)
     energy[...] = total
 
@@ -162,7 +162,7 @@
                 device_id=(me_c, y * NX + lax.rem(x + d, NX)), device_id_type=MESH,
             ).start()
 
-    for d in (4, 3, 5, 2, 6, 1, 7):
+    for d in (1, 7, 2, 6, 3, 5, 4):
         pltpu.make_async_remote_copy(
             src_ref=own, dst_ref=own, send_sem=y_send, recv_sem=y_recv.at[NY - d],
             device_id=(me_c, lax.rem(y + d, NY) * NX + x), device_id_type=MESH,
@@ -177,8 +177,9 @@
     table = jnp.concatenate([table_ref[...], jnp.zeros((WIDE - CYCLES, BINS), F32)], axis=0)
     ctf = lax.dot_general(bin_hot, table, nt, precision=HIGH, preferred_element_type=F32)
     penalty = 0.5 * lax.dot_general(
-        ctf * ctf, energy[...], nt, precision=HIGH, preferred_element_type=F32
-    )
+        energy[...], ctf * ctf, nt, precision=HIGH, preferred_element_type=F32
+    )
+    penalty = jnp.concatenate([penalty] * HALF, axis=1)
 
     for rho in (1, 7, 2, 6, 3, 5, 4):
         settle(grid.at[0, 0], y_recv.at[rho])
@@ -208,7 +209,7 @@
     rest = jnp.concatenate([rest[:, t * WIDE : (t + 1) * WIDE] for t in range(CAP)], axis=0)
 
     def turn(block, at):
-        for r in range(ROTS):
+        for r in range(HALF):
             lhs[r * SLOTS : (r + 1) * SLOTS, at * WIDE : (at + 1) * WIDE] = pltpu.roll(
                 block, r * STEP, 1
             )
@@ -231,7 +232,7 @@
         for c in range(NX):
             turn(cycle(row * NX + c), c)
         term = lax.dot_general(
-            lhs[...], tbuf[:, row * NX * WIDE : (row + 1) * NX * WIDE], nt,
+            tbuf[:, row * NX * WIDE : (row + 1) * NX * WIDE], lhs[...], nt,
             preferred_element_type=F32,
         )
         if row == 0:
@@ -240,13 +241,13 @@
             acc[...] += term
     turn(cycle(NDIR), 0)
     cross = acc[...] + lax.dot_general(
-        lhs[:, :WIDE], tbuf[:, NDIR * WIDE :], nt, preferred_element_type=F32
-    )
-    top = cross[:SLOTS]
-    for r in range(1, ROTS):
-        top = jnp.maximum(top, cross[r * SLOTS : (r + 1) * SLOTS])
-    local = jnp.max((top - penalty) * SCALE, axis=1, keepdims=True)
-    local = to_row(local, SLOTS, WIDE)
+        tbuf[:, NDIR * WIDE :], lhs[:, :WIDE], nt, preferred_element_type=F32
+    )
+    top = jnp.maximum(cross[:dirs], cross[dirs:]) - penalty
+    local = jnp.max(top, axis=0, keepdims=True) * SCALE
+    for r in (4, 2, 1):
+        local = jnp.maximum(local[:, : r * SLOTS], local[:, r * SLOTS :])
+    local = jnp.concatenate([local, jnp.zeros((1, WIDE - SLOTS), F32)], axis=1)
 
     dsend[...] = local
     dbuf[me_d] = local
@@ -264,7 +265,7 @@
     answer = jnp.where(lanes == SLOTS, squares, group)
     esend[...] = answer
     ebuf[me_c] = answer
-    for d in (8, 9, 7, 10, 6, 11, 5, 12, 4, 13, 3, 14, 2, 15, 1):
+    for d in OUTWARD:
         pltpu.make_async_remote_copy(
             src_ref=esend, dst_ref=ebuf.at[me_c], send_sem=e_send, recv_sem=e_recv,
             device_id=(lax.rem(me_c + d, NCLS), me_d), device_id_type=MESH,
@@ -300,14 +301,14 @@
         pltpu.VMEM((1, ROWS), I32),
         pltpu.VMEM((1, ROWS), I32),
         pltpu.VMEM((CYCLES, BINS), F32),
-        pltpu.VMEM((dirs, FEAT), BF16),
+        pltpu.VMEM((2 * dirs, FEAT), BF16),
         pltpu.VMEM((dirs, WIDE), F32),
         pltpu.VMEM((NCLS * ROWS, WIDE), BF16),
         pltpu.VMEM((NCLS * ROWS, WIDE), BF16),
         pltpu.VMEM((NY, NX, 4 * ROWS, WIDE), BF16),
         pltpu.VMEM((NX, ROWS, WIDE), BF16),
-        pltpu.VMEM((ROTS * SLOTS, NX * WIDE), BF16),
-        pltpu.VMEM((ROTS * SLOTS, dirs), F32),
+        pltpu.VMEM((HALF * SLOTS, NX * WIDE), BF16),
+        pltpu.VMEM((2 * dirs, HALF * SLOTS), F32),
         pltpu.VMEM((1, WIDE), F32),
         pltpu.VMEM((NDIR, 1, WIDE), F32),
         pltpu.VMEM((1, WIDE), F32),

time: 46.2 us -> 45.1 us (0.976)
  Pallas kernels: 44.2 us -> 43.1 us
    pallas_call x1, Pallas kernels: 44.2 us -> 43.1 us  [on_device(): pl.pallas_call(kernel, out_shape=jax.ShapeDtypeStruct((2, ROWS), F32), in...]
where the time goes in v3:
time: 45.1 us; the launch traced here: 45 us
  Pallas kernels  43.1 us (96%)
  local copies, waits for them, and re-layouts  1.25 us (3%)
  between operations  0.64 us (1%)
    pallas_call x1, Pallas kernels, on_device(): pl.pallas_call(kernel, out_shape=jax.ShapeDtypeStruct((2, ROWS), F32), in...  43.1 us
    squeeze x1, local copies, waits for them, and re-layouts, on_device(): return (out[0], out[1])  1.25 us

profile of v3, /device:TPU:1, one launch (start us, length us, event | category | flops | bytes accessed | tf_op | source)
XLA Modules:
  0.0 45.0 jit_solution(16655973372825565750)
XLA Ops:
  0.6 43.1 %shard_map.68 = f32[2,16]{1,0:T(2,128)} custom-call(bf16[16,132]{1,0:T(8,128)(2,1)} %part_hbm.1, s32[1,16]{1,0:T(1,128)} %bitcast.8, s32[1,16]{1,0:T(1,128)} %bitcast.9, f32[33,64]{1,0:T(8,128)} %bitcast.7, bf16[1,144,4224]{2,1,0:T(8,128)(2,1)} %refs_hbm.1), custom_call_target="tpu_custom_call" | custom-call | tf_op jit(solution)/shard_map/pallas_call | solution.py:319
  43.7 1.3 %slice_bitcast_fusion = (f32[16]{0:T(128)}, f32[16]{0:T(128)}) fusion(f32[2,16]{1,0:T(2,128)} %shard_map.68), kind=kLoop, calls=%fused_computation | loop fusion | bytes 256 | tf_op jit(solution)/shard_map/squeeze | solution.py:335

commit v4 on v3

--- a/solution.py
+++ b/solution.py
@@ -57,7 +57,7 @@
     part_hbm, assign_hbm, bins_hbm, table_hbm, refs_hbm, out_ref,
     part_ref, assign_ref, bins_ref, table_ref, tbuf, energy, bsend, brecv,
     grid, aux4, lhs, acc, dsend, dbuf, esend, ebuf,
-    in_sem, load_sem, b_send, b_recv, y_send, y_recv, x_send, x_recv, u_send, u_recv,
+    in_sem, load_sem, b_send, b_recv, y_send, y_recv, x_send, x_recv, w_send, w_recv, u_send, u_recv,
     d_send, d_recv, e_send, e_recv,
 ):
     me_c = lax.axis_index("cls")
@@ -150,8 +150,9 @@
     b_all = brecv.at[pl.ds(0, (NCLS - 1) * ROWS)]
     settle(b_all, b_recv)
     unpacked = jnp.dot(unpack, brecv[...], preferred_element_type=F32)
-    own = grid.at[y, x]
-    own[...] = unpacked.astype(BF16)
+    grid[y, x] = unpacked.astype(BF16)
+    own = grid.at[y, x, pl.ds(0, SLOTS)]
+    own_aux = grid.at[y, x, pl.ds(SLOTS, ROWS)]
 
     def forward(rho):
         row = lax.rem(y + rho, NY)
@@ -162,6 +163,11 @@
                 device_id=(me_c, y * NX + lax.rem(x + d, NX)), device_id_type=MESH,
             ).start()
 
+    for d in (4, 3, 5, 2, 6, 1, 7):
+        pltpu.make_async_remote_copy(
+            src_ref=own_aux, dst_ref=own_aux, send_sem=w_send, recv_sem=w_recv,
+            device_id=(me_c, lax.rem(y + d, NY) * NX + x), device_id_type=MESH,
+        ).start()
     for d in (1, 7, 2, 6, 3, 5, 4):
         pltpu.make_async_remote_copy(
             src_ref=own, dst_ref=own, send_sem=y_send, recv_sem=y_recv.at[NY - d],
@@ -181,9 +187,13 @@
     )
     penalty = jnp.concatenate([penalty] * HALF, axis=1)
 
-    for rho in (1, 7, 2, 6, 3, 5, 4):
-        settle(grid.at[0, 0], y_recv.at[rho])
-        forward(rho)
+    def pass_on(rows):
+        for rho in rows:
+            settle(own, y_recv.at[rho])
+            forward(rho)
+
+    pass_on((1, 7))
+    settle(grid.at[pl.ds(0, 7), 0, pl.ds(0, ROWS)], w_recv)
     over = jnp.zeros((ROWS, WIDE), F32)
     for row in range(NY):
         over = over + grid[row, x, SLOTS:, :].astype(F32)
@@ -194,14 +204,13 @@
             device_id=(me_c, y * NX + lax.rem(x + d, NX)), device_id_type=MESH,
         ).start()
 
+    pass_on((2, 6, 3, 5, 4))
+
     at = iota((1, CAP * WIDE), 1)
     place, at = at >> 7, at & (WIDE - 1)
     spread_to = ((at >> 2) & 3) * WIDE + (at >> 4) * 12 + place * 4 + (at & 3)
     spreading = (iota((NX * WIDE, CAP * WIDE), 0) == spread_to).astype(F32).astype(BF16)
 
-    for rho in (0, 1, 7, 2, 6, 3, 5, 4):
-        for d in range(1, NX):
-            settle(grid.at[0, 0, pl.ds(0, SLOTS)], x_recv.at[d, rho])
     settle(aux4.at[pl.ds(0, 3)], u_recv)
 
     rest = jnp.concatenate([aux4[c] for c in range(NX)], axis=1)
@@ -217,29 +226,32 @@
     def select(low, high):
         return ((lanes >= low) & (lanes < high)).astype(F32).astype(BF16)
 
-    def cycle(k):
-        block = None
-        if k < NDIR:
-            block = grid[k // NX, k % NX, :SLOTS, :] * select(4 * k, WIDE)
-        if k > 0:
-            j = k - 1
-            early = grid[j // NX, j % NX, :SLOTS, :] * select(0, 4 * j)
-            early = early + rest * select(4 * j, 4 * k)
-            block = early if block is None else block + early
-        return block
-
-    for row in range(NY):
+    def early(row, c, j):
+        return grid[row, c, :SLOTS, :] * select(0, 4 * j) + rest * select(4 * j, 4 * j + 4)
+
+    def add_row(rho):
+        row = lax.rem(y + rho, NY)
         for c in range(NX):
-            turn(cycle(row * NX + c), c)
+            k = row * NX + c
+            before = (row, c - 1) if c else (lax.rem(row + NY - 1, NY), NX - 1)
+            turn(grid[row, c, :SLOTS, :] * select(4 * k, WIDE) + early(*before, k - 1), c)
         term = lax.dot_general(
-            tbuf[:, row * NX * WIDE : (row + 1) * NX * WIDE], lhs[...], nt,
+            tbuf[:, pl.ds(pl.multiple_of(row * NX * WIDE, NX * WIDE), NX * WIDE)], lhs[...], nt,
             preferred_element_type=F32,
         )
-        if row == 0:
+        if rho == 0:
             acc[...] = term
         else:
             acc[...] += term
-    turn(cycle(NDIR), 0)
+
+    for rho, ready in (
+        (0, ()), (7, (0,)), (1, (1,)), (6, (7,)), (2, (2,)), (5, (6,)), (3, (3,)), (4, (4, 5))
+    ):
+        for d in range(1, NX):
+            settle(grid.at[0, 0, pl.ds(0, SLOTS)], x_recv.at[d, rho])
+        for r in ready:
+            add_row(r)
+    turn(early(NY - 1, NX - 1, NDIR - 1), 0)
     cross = acc[...] + lax.dot_general(
         tbuf[:, NDIR * WIDE :], lhs[:, :WIDE], nt, preferred_element_type=F32
     )
@@ -271,7 +283,8 @@
             device_id=(lax.rem(me_c + d, NCLS), me_d), device_id_type=MESH,
         ).start()
     settle(b_all, b_send)
-    settle(grid.at[pl.ds(0, 7), 0], y_send)
+    settle(grid.at[pl.ds(0, 7), 0, pl.ds(0, SLOTS)], y_send)
+    settle(grid.at[pl.ds(0, 7), 0, pl.ds(0, ROWS)], w_send)
     settle(grid.at[pl.ds(0, NY), pl.ds(0, 3), pl.ds(0, SLOTS)], x_send)
     settle(aux4.at[pl.ds(0, 3)], u_send)
     settle(d_all, d_send)
@@ -315,7 +328,7 @@
         pltpu.VMEM((NCLS, 1, WIDE), F32),
     ]
     dma = pltpu.SemaphoreType.DMA
-    sems = [dma((4,)), dma, dma, dma, dma, dma((NY,)), dma, dma((NX, NY))] + [dma] * 6
+    sems = [dma((4,)), dma, dma, dma, dma, dma((NY,)), dma, dma((NX, NY))] + [dma] * 8
     out = pl.pallas_call(
         kernel,
         out_shape=jax.ShapeDtypeStruct((2, ROWS), F32),

time: 45.1 us -> 44.3 us (0.982)
  Pallas kernels: 43.1 us -> 42.3 us
    pallas_call x1, Pallas kernels: 43.1 us -> 42.3 us  [on_device(): pl.pallas_call(kernel, out_shape=jax.ShapeDtypeStruct((2, ROWS), F32), in...]
where the time goes in v4:
time: 44.3 us; the launch traced here: 44.2 us
  Pallas kernels  42.3 us (95%)
  local copies, waits for them, and re-layouts  1.25 us (3%)
  between operations  0.64 us (1%)
    pallas_call x1, Pallas kernels, on_device(): pl.pallas_call(kernel, out_shape=jax.ShapeDtypeStruct((2, ROWS), F32), in...  42.3 us
    squeeze x1, local copies, waits for them, and re-layouts, on_device(): return (out[0], out[1])  1.25 us

profile of v4, /device:TPU:1, one launch (start us, length us, event | category | flops | bytes accessed | tf_op | source)
XLA Modules:
  0.0 44.2 jit_solution(16682946713999088363)
XLA Ops:
  0.6 42.3 %shard_map.68 = f32[2,16]{1,0:T(2,128)} custom-call(bf16[16,132]{1,0:T(8,128)(2,1)} %part_hbm.1, s32[1,16]{1,0:T(1,128)} %bitcast.8, s32[1,16]{1,0:T(1,128)} %bitcast.9, f32[33,64]{1,0:T(8,128)} %bitcast.7, bf16[1,144,4224]{2,1,0:T(8,128)(2,1)} %refs_hbm.1), custom_call_target="tpu_custom_call" | custom-call | tf_op jit(solution)/shard_map/pallas_call | solution.py:332
  42.9 1.3 %slice_bitcast_fusion = (f32[16]{0:T(128)}, f32[16]{0:T(128)}) fusion(f32[2,16]{1,0:T(2,128)} %shard_map.68), kind=kLoop, calls=%fused_computation | loop fusion | bytes 256 | tf_op jit(solution)/shard_map/squeeze | solution.py:348
